TPU v7x, 32 devices: a whole 2x2x4 slice. The times are simulated.
32 devices in a mesh: gx: 4 (over y, x), gy: 8 (over z, core).
Axes of the slice: x: 2, y: 2, z: 4, core: 2. Of those that a mesh axis runs over, the one named last changes fastest.
Arguments:
- e_field: float32 [3, 32, 256, 512], P(None, 'gx', 'gy'), may hold values from -6 to 6
- h_field: float32 [3, 32, 256, 512], P(None, 'gx', 'gy'), may hold values from -6 to 6
- polar: float32 [3, 32, 256, 512], P(None, 'gx', 'gy'), may hold values from -6 to 6
- polar_prev: float32 [3, 32, 256, 512], P(None, 'gx', 'gy'), may hold values from -6 to 6
- material: int32 [32, 256, 512], P('gx', 'gy'), may hold values from 0 to 3
- eps_table: float32 [4], replicated, may hold values from 1 to 6
- delta_table: float32 [4], replicated, may hold values from 0.5 to 4
- omega_table: float32 [4], replicated, may hold values from 0.2 to 1.2
- damping_table: float32 [4], replicated, may hold values from 0.02 to 0.6
- surface_flags: int32 [4, 8], P('gx', 'gy'), may hold values 0 or 1
Outputs:
- e_out: float32 [3, 32, 256, 512], P(None, 'gx', 'gy')
- h_out: float32 [3, 32, 256, 512], P(None, 'gx', 'gy')
- polar_out: float32 [3, 32, 256, 512], P(None, 'gx', 'gy')
- far_field: float32 [2, 2, 4, 16384], replicated
All inputs are finite; a program needn't handle non-finite values. No bound on the sum of `surface_flags` on one device may be relied on, other than what follows from the above.
Results may differ from a plain program's by a relative error of at most 0.0003.
Values sent between devices are 32-bit elements; how exact they have to be, the bound alone decides.
A program may use at most 256 MiB of HBM per device.

v0:
```python
import math
import jax
import jax.numpy as jnp
from jax import lax
from jax.sharding import PartitionSpec as P

NTH = 64
NPH = 256
NDIR = 16384
ZS = 384
DT = 0.55
WAVELENGTHS = (5.0, 4.0)


def shifted(shard, axis, by):
    peers = lax.axis_size(axis)
    pairs = [(i, i + by) for i in range(peers) if 0 <= i + by < peers]
    return lax.ppermute(shard, axis, pairs)


def ahead(field, plane, axis):
    rest = lax.slice_in_dim(field, 1, field.shape[axis], axis=axis)
    return jnp.concatenate([rest, plane], axis=axis) - field


def behind(field, plane, axis):
    rest = lax.slice_in_dim(field, 0, field.shape[axis] - 1, axis=axis)
    return field - jnp.concatenate([plane, rest], axis=axis)


def zero_plane(field, axis):
    shape = list(field.shape)
    shape[axis] = 1
    return jnp.zeros(shape, jnp.float32)


def coefficients(eps_table, delta_table, omega_table, damping_table):
    half = damping_table * (DT / 2.0)
    denom = 1.0 + half
    square = omega_table * omega_table * (DT * DT)
    return (
        (2.0 - square) / denom,
        (half - 1.0) / denom,
        delta_table * square / denom,
        1.0 / eps_table,
    )


def curl_e(ex, ey, ez, xnext, ynext):
    zplane = zero_plane(ex, 2)
    curl_x = ahead(ez, ynext[1], 1) - ahead(ey, zplane, 2)
    curl_y = ahead(ex, zplane, 2) - ahead(ez, xnext[1], 0)
    curl_z = ahead(ey, xnext[0], 0) - ahead(ex, ynext[0], 1)
    return (curl_x, curl_y, curl_z)


def curl_h(hx, hy, hz, xprev, yprev):
    zplane = zero_plane(hx, 2)
    curl_x = behind(hz, yprev[1], 1) - behind(hy, zplane, 2)
    curl_y = behind(hx, zplane, 2) - behind(hz, xprev[1], 0)
    curl_z = behind(hy, xprev[0], 0) - behind(hx, yprev[0], 1)
    return (curl_x, curl_y, curl_z)


def directions(start, count):
    index = start + jnp.arange(count, dtype=jnp.int32)
    theta = ((index // NPH).astype(jnp.float32) + 0.5) * (math.pi / 2.0 / NTH)
    phi = ((index % NPH).astype(jnp.float32) + 0.5) * (2.0 * math.pi / NPH)
    return (jnp.sin(theta) * jnp.cos(phi), jnp.sin(theta) * jnp.sin(phi))


def lookup(material, table, count):
    result = jnp.zeros(material.shape, jnp.float32)
    for index in range(count):
        result = result + jnp.where(material == index, table[index], 0.0)
    return result


def next_planes(ex, ey, ez):
    xface = shifted(jnp.stack([ey[:1], ez[:1]]), "gx", -1)
    yface = shifted(jnp.stack([ex[:, :1], ez[:, :1]]), "gy", -1)
    return ((xface[0], xface[1]), (yface[0], yface[1]))


def prev_planes(hx, hy, hz):
    xface = shifted(jnp.stack([hy[-1:], hz[-1:]]), "gx", 1)
    yface = shifted(jnp.stack([hx[:, -1:], hz[:, -1:]]), "gy", 1)
    return ((xface[0], xface[1]), (yface[0], yface[1]))


def project_cells(real_acc, imag_acc, xvalues, yvalues, start, count):
    rows_x = xvalues.shape[0]
    rows_y = yvalues.shape[0]
    cells = rows_x * rows_y
    real_flat = real_acc.reshape(2, 4, cells)
    imag_flat = imag_acc.reshape(2, 4, cells)
    width = math.gcd(count, 2048)
    blocks = count // width

    def project(offset):
        dir_x, dir_y = directions(start + offset, width)
        parts = []
        for f in range(2):
            wave = 2.0 * math.pi / WAVELENGTHS[f]
            along_x = wave * xvalues[:, None] * dir_x[None, :]
            along_y = wave * yvalues[:, None] * dir_y[None, :]
            cos_x = jnp.cos(along_x)
            sin_x = jnp.sin(along_x)
            cos_y = jnp.cos(along_y)
            sin_y = jnp.sin(along_y)
            cosine = (
                cos_x[:, None, :] * cos_y[None, :, :] - sin_x[:, None, :] * sin_y[None, :, :]
            ).reshape(cells, width)
            sine = (
                sin_x[:, None, :] * cos_y[None, :, :] + cos_x[:, None, :] * sin_y[None, :, :]
            ).reshape(cells, width)
            hi = lax.Precision.HIGHEST
            real_part = jnp.dot(real_flat[f], cosine, precision=hi) - jnp.dot(
                imag_flat[f], sine, precision=hi
            )
            imag_part = jnp.dot(real_flat[f], sine, precision=hi) + jnp.dot(
                imag_flat[f], cosine, precision=hi
            )
            parts.append(jnp.stack([real_part, imag_part]))
        return jnp.stack(parts)

    offsets = jnp.arange(blocks, dtype=jnp.int32) * width
    pieces = lax.map(project, offsets)
    return jnp.moveaxis(pieces, 0, 3).reshape(2, 2, 4, count)


def shards(
    e_field,
    h_field,
    polar,
    polar_prev,
    material,
    eps_table,
    delta_table,
    omega_table,
    damping_table,
    surface_flags,
):
    cells_x = e_field.shape[1]
    cells_y = e_field.shape[2]
    count = eps_table.shape[0]
    coef_a, coef_b, coef_c, coef_inv = coefficients(
        eps_table, delta_table, omega_table, damping_table
    )
    vox_a = lookup(material, coef_a, count)
    vox_b = lookup(material, coef_b, count)
    vox_c = lookup(material, coef_c, count)
    vox_inv = lookup(material, coef_inv, count)
    flag = surface_flags[0, 0].astype(jnp.float32)
    ex, ey, ez = (e_field[0], e_field[1], e_field[2])
    hx, hy, hz = (h_field[0], h_field[1], h_field[2])
    pols = [polar[0], polar[1], polar[2]]
    prevs = [polar_prev[0], polar_prev[1], polar_prev[2]]
    real_acc = jnp.zeros((2, 4, cells_x, cells_y), jnp.float32)
    imag_acc = jnp.zeros((2, 4, cells_x, cells_y), jnp.float32)
    for step in range(2):
        xnext, ynext = next_planes(ex, ey, ez)
        curl_x, curl_y, curl_z = curl_e(ex, ey, ez, xnext, ynext)
        hx = hx - DT * curl_x
        hy = hy - DT * curl_y
        hz = hz - DT * curl_z
        fields = [ex, ey, ez]
        newpol = [vox_a * pols[i] + vox_b * prevs[i] + vox_c * fields[i] for i in range(3)]
        xprev, yprev = prev_planes(hx, hy, hz)
        curls = curl_h(hx, hy, hz, xprev, yprev)
        fields = [fields[i] + (DT * curls[i] - (newpol[i] - pols[i])) * vox_inv for i in range(3)]
        ex, ey, ez = fields
        prevs = pols
        pols = newpol
        surface = jnp.stack([-hy[:, :, ZS], hx[:, :, ZS], ey[:, :, ZS], -ex[:, :, ZS]]) * flag
        moment = (step + 1) * DT
        real_acc = real_acc + jnp.stack(
            [surface * math.cos(2.0 * math.pi / WAVELENGTHS[f] * moment) for f in range(2)]
        )
        imag_acc = imag_acc - jnp.stack(
            [surface * math.sin(2.0 * math.pi / WAVELENGTHS[f] * moment) for f in range(2)]
        )
    xglobal = (lax.axis_index("gx") * cells_x + jnp.arange(cells_x, dtype=jnp.int32)).astype(
        jnp.float32
    )
    yglobal = (lax.axis_index("gy") * cells_y + jnp.arange(cells_y, dtype=jnp.int32)).astype(
        jnp.float32
    )
    partial_far = project_cells(real_acc, imag_acc, xglobal, yglobal, 0, NDIR)
    total = lax.psum(partial_far, ("gx", "gy"))
    grid_x = cells_x * lax.axis_size("gx")
    grid_y = cells_y * lax.axis_size("gy")
    far_field = total * (1.0 / math.sqrt(grid_x * grid_y))
    return (jnp.stack([ex, ey, ez]), jnp.stack([hx, hy, hz]), jnp.stack(pols), far_field)


def solution(mesh):
    placed = (
        P(None, "gx", "gy", None),
        P(None, "gx", "gy", None),
        P(None, "gx", "gy", None),
        P(None, "gx", "gy", None),
        P("gx", "gy", None),
        P(),
        P(),
        P(),
        P(),
        P("gx", "gy"),
    )
    return jax.shard_map(
        shards,
        mesh=mesh,
        in_specs=placed,
        out_specs=(
            P(None, "gx", "gy", None),
            P(None, "gx", "gy", None),
            P(None, "gx", "gy", None),
            P(),
        ),
        check_vma=False,
    )
```

profile of v0, /device:TPU:0, one launch (start us, length us, event | category | flops | bytes accessed | tf_op | source)
XLA Modules:
  0.0 399.2 jit_solution(10119303926188444393)
XLA Ops:
  7.3 1.6 slice_bitcast_fusion.1
  9.0 1.3 collective-permute-start.1
  10.3 1.3 collective-permute-start
  19.7 3.1 fusion.46
  23.1 3.0 collective-permute-start.2
  28.5 6.1 %collective-permute-start.3 = (f32[2,1,32,512]{3,2,1,0:T(8,128)}, f32[2,1,32,512]{3,2,1,0:T(8,128)}, u32[]{:S(2)}, u32[]{:S(2)}) collective-permute-start(f32[2,1,32,512]{3,2,1,0:T(8,128)} %pad_maximum_fusion.3), channel_id=1, source_target_pairs={{0,8},{8,16},{16,24},{1,9},{9,17},{17,25},{2,10},{10,18},{18,26},{... | collective-permute-start | bytes 393224 | tf_op jit(solution)/shard_map/ppermute | solution.py:18
  35.9 13.2 %fusion.51 = (f32[8,32,512]{2,1,0:T(8,128)S(1)}, f32[8,32,512]{2,1,0:T(8,128)}, pred[8,32,512]{2,1,0:T(8,128)(4,1)S(1)}, pred[8,32,512]{2,1,0:T(8,128)(4,1)S(1)}...) fusion(f32[8,32,512]{2,1,0:T(8,128)S(1)} %get-tuple-element.169, f32[8,31,512]{2,1,0:T(8,128)S(1)} %bitcast.335, ...), kind=kLoop, calls=%fused_computation.90 | loop fusion | flops 6029312 | bytes 5766208 | tf_op jit(solution)/shard_map/add | solution.py:171
  51.7 1.3 stack.241
  54.8 13.0 %fusion.64 = (f32[8,32,512]{2,1,0:T(8,128)S(1)}, f32[8,32,512]{2,1,0:T(8,128)}) fusion(f32[8,32,512]{2,1,0:T(8,128)S(1)} %get-tuple-element.170, f32[7,32,512]{2,1,0:T(8,128)} %slice.432, f32[1,32,512]{2,1,0:T(8,128)S(1)} %get-tuple-element.184, f32[8,32,512]{2,1,0:T(8,128)S(1)} %get-tuple-element.168, f32[8,31,512]{2,1,0:T(8,128)S(1)} %bitcast.328, ...), kind=kLoop, calls=%fused_computation.106 | loop fusion | flops 5636096 | bytes 5242944 | tf_op jit(solution)/shard_map/add | solution.py:171
  68.7 12.8 %fusion.59 = (f32[8,32,512]{2,1,0:T(8,128)S(1)}, f32[8,32,512]{2,1,0:T(8,128)}) fusion(f32[8,32,512]{2,1,0:T(8,128)S(1)} %get-tuple-element.169, f32[7,32,512]{2,1,0:T(8,128)S(1)} %copy-done.22, f32[1,32,512]{2,1,0:T(8,128)S(1)} %get-tuple-element.183, f32[8,32,512]{2,1,0:T(8,128)S(1)} %get-tuple-element.168, f32[8,32,511]{2,1,0:T(8,128)S(1)} %bitcast.329, ...), kind=kLoop, calls=%fused_computation.100 | loop fusion | flops 5505024 | bytes 5241920 | tf_op jit(solution)/shard_map/add | solution.py:171
  82.5 1.4 collective-permute-start.5
  85.6 1.3 slice.441
  86.8 1.2 slice.443
  88.2 1.3 collective-permute-start.4
  89.5 5.8 %collective-permute-done.4 = f32[2,1,32,512]{3,2,1,0:T(8,128)S(1)} collective-permute-done((f32[2,1,32,512]{3,2,1,0:T(8,128)S(1)}, f32[2,1,32,512]{3,2,1,0:T(8,128)S(1)}, u32[]{:S(2)}, u32[]{:S(2)}) %collective-permute-start.4) | collective-permute-done | bytes 131104 | tf_op jit(solution)/shard_map/ppermute | solution.py:18
  96.5 2.9 collective-permute-start.6
  99.4 1.3 pad_maximum_fusion.1
  102.3 4.8 %collective-permute-start.7 = (f32[2,1,32,512]{3,2,1,0:T(8,128)S(1)}, f32[2,1,32,512]{3,2,1,0:T(8,128)S(1)}, u32[]{:S(2)}, u32[]{:S(2)}) collective-permute-start(f32[2,1,32,512]{3,2,1,0:T(8,128)S(1)} %pad_maximum_fusion.5), channel_id=1, source_target_pairs={{0,8},{8,16},{16,24},{1,9},{9,17},{17,25},{2,10},{10,18},{18,26},{... | collective-permute-start | bytes 393224 | tf_op jit(solution)/shard_map/ppermute | solution.py:18
  107.3 12.9 %fusion.75 = (f32[8,32,512]{2,1,0:T(8,128)S(1)}, f32[8,32,512]{2,1,0:T(8,128)}) fusion(f32[8,32,512]{2,1,0:T(8,128)S(1)} %copy-done.3, f32[8,32,512]{2,1,0:T(8,128)S(1)} %get-tuple-element.177, f32[8,31,512]{2,1,0:T(8,128)S(1)} %bitcast.334, f32[8,1,512]{2,1,0:T(1,128)S(1)} %get-tuple-element.187, f32[8,32,512]{2,1,0:T(8,128)} %get-tuple-element.137, ...), kind=kLoop, calls=%fused_computation.122 | loop fusion | flops 5505024 | bytes 5241920 | tf_op jit(solution)/shard_map/add | solution.py:171
  121.3 12.9 %fusion.83 = (f32[8,32,512]{2,1,0:T(8,128)S(1)}, f32[8,32,512]{2,1,0:T(8,128)}) fusion(f32[8,32,512]{2,1,0:T(8,128)S(1)} %copy-done.7, f32[8,32,512]{2,1,0:T(8,128)S(1)} %get-tuple-element.177, f32[7,32,512]{2,1,0:T(8,128)} %slice.456, f32[1,32,512]{2,1,0:T(8,128)S(1)} %get-tuple-element.179, f32[8,32,512]{2,1,0:T(8,128)} %get-tuple-element.143, ...), kind=kLoop, calls=%fused_computation.132 | loop fusion | flops 5505024 | bytes 5241920 | tf_op jit(solution)/shard_map/add | solution.py:171
  135.0 122.4 %while.13 = (s32[]{:T(128)}, f32[8,2,2,4,2048]{4,3,2,1,0:T(4,128)}, s32[8]{0:T(128)S(1)}, f32[2,4,256]{2,1,0:T(4,128)S(1)}, f32[2,4,256]{2,1,0:T(4,128)S(1)}, /*index=5*/s32[]{:T(128)}, s32[]{:T(128)}, s32[]{:T(128)}) while((s32[]{:T(128)}, f32[8,2,2,4,2048]{4,3,2,1,0:T(4,128)}, s32[8]{0:T(128)S(1)}, f32[2,4,256]{2,1,0:T(4,128)S(1)}, ...), condition=%wide.region_1.2_spmd.clone, body=%wide.region_0.1_spmd.clone.sunk | while | flops 207937696 | bytes 28771064 | solution.py:128
  136.4 1.9 multiply_cosine_fusion.6
  140.6 1.2 fusion.167
  141.8 1.2 fusion.168
  143.0 1.2 fusion.169
  146.0 1.2 fusion.171
  147.2 1.2 fusion.172
  148.4 1.2 fusion.173
  151.7 1.9 multiply_cosine_fusion.6
  155.9 1.2 fusion.167
  157.1 1.2 fusion.168
  161.3 1.2 fusion.171
  162.5 1.2 fusion.172
  163.7 1.2 fusion.173
  167.0 1.9 multiply_cosine_fusion.6
  171.2 1.2 fusion.167
  172.4 1.2 fusion.168
  173.6 1.2 fusion.169
  176.6 1.2 fusion.171
  177.8 1.2 fusion.172
  179.0 1.2 fusion.173
  182.3 1.9 multiply_cosine_fusion.6
  186.5 1.2 fusion.167
  187.7 1.2 fusion.168
  188.9 1.2 fusion.169
  193.1 1.2 fusion.172
  197.6 1.9 multiply_cosine_fusion.6
  203.0 1.2 fusion.168
  208.4 1.2 fusion.172
  212.9 1.9 multiply_cosine_fusion.6
  218.3 1.2 fusion.168
  223.7 1.2 fusion.172
  228.2 1.9 multiply_cosine_fusion.6
  233.6 1.2 fusion.168
  239.0 1.2 fusion.172
  243.5 1.9 multiply_cosine_fusion.6
  248.9 1.2 fusion.168
  254.3 1.2 fusion.172
  257.4 2.4 copy.16
  259.9 12.3 %fusion.89 = (f32[1,8,32,512]{3,2,1,0:T(8,128)S(1)}, f32[8,32,512]{2,1,0:T(8,128)S(1)}) fusion(f32[8,32,512]{2,1,0:T(8,128)S(1)} %copy-done.11, f32[8,32,512]{2,1,0:T(8,128)S(1)} %get-tuple-element.178, f32[7,32,512]{2,1,0:T(8,128)} %slice.458, f32[1,32,512]{2,1,0:T(8,128)S(1)} %get-tuple-element.180, f32[8,32,512]{2,1,0:T(8,128)S(1)} %get-tuple-element.176, ...), kind=kLoop, calls=%fused_computation.139 | loop fusion | flops 5636096 | bytes 5242944 | tf_op jit(solution)/shard_map/stack | solution.py:194
  272.2 1.3 pad_maximum_fusion
  273.7 1.3 pad_maximum_fusion.2
  275.0 115.0 %all-reduce.10.cloned.1.call-done = f32[2,2,4,16384]{3,2,1,0:T(4,128)} async-done(((f32[2,2,4,16384]{3,2,1,0:T(4,128)}), f32[2,2,4,16384]{3,2,1,0:T(4,128)}) %all-reduce.10.cloned.1.call-update) | async-done | bytes 1048592 | tf_op jit(solution)/shard_map/psum | solution.py:190
  389.9 2.5 broadcast_multiply_fusion
  (263 shorter events, 96.3 us)
Async XLA Ops:
  7.2 3.1 copy-start
  7.2 5.5 %copy-start.33 = (f32[4]{0:T(128)S(1)}, f32[4]{0:T(128)}, u32[]{:S(2)}) copy-start(f32[4]{0:T(128)} %param.17) | copy-start | bytes 52
  7.2 6.2 %copy-start.30 = (f32[4]{0:T(128)S(1)}, f32[4]{0:T(128)}, u32[]{:S(2)}) copy-start(f32[4]{0:T(128)} %param.19) | copy-start | bytes 52
  7.2 6.1 %copy-start.31 = (f32[4]{0:T(128)S(1)}, f32[4]{0:T(128)}, u32[]{:S(2)}) copy-start(f32[4]{0:T(128)} %param.20) | copy-start | bytes 52
  7.2 6.1 %copy-start.32 = (f32[4]{0:T(128)S(1)}, f32[4]{0:T(128)}, u32[]{:S(2)}) copy-start(f32[4]{0:T(128)} %param.18) | copy-start | bytes 52
  7.2 382.7 %all-reduce.10.cloned.1.call-start = ((), (), s32[]{:S(2)}) async-start(), calls=%async_computation | async-start | bytes 2097152 | tf_op jit(solution)/shard_map/psum | solution.py:190
  9.0 10.7 %collective-permute-start.1 = (f32[2,8,1,512]{3,2,1,0:T(1,128)S(1)}, f32[2,8,1,512]{3,2,1,0:T(1,128)S(1)}, u32[]{:S(2)}, u32[]{:S(2)}) collective-permute-start(f32[2,8,1,512]{3,2,1,0:T(1,128)S(1)} %pad_maximum_fusion.6), channel_id=1, source_target_pairs={{1,0},{2,1},{3,2},{4,3},{5,4},{6,5},{7,6},{9,8},{10,9},{11,10},{12... | collective-permute-start | bytes 98312 | tf_op jit(solution)/shard_map/ppermute | solution.py:18
  10.3 9.4 %collective-permute-start = (f32[2,1,32,512]{3,2,1,0:T(8,128)S(1)}, f32[2,1,32,512]{3,2,1,0:T(8,128)S(1)}, u32[]{:S(2)}, u32[]{:S(2)}) collective-permute-start(f32[2,1,32,512]{3,2,1,0:T(8,128)S(1)} %stack.204), channel_id=1, source_target_pairs={{8,0},{16,8},{24,16},{9,1},{17,9},{25,17},{10,2},{18,10},{26,18},{... | collective-permute-start | bytes 393224 | tf_op jit(solution)/shard_map/ppermute | solution.py:18
  23.1 12.8 %collective-permute-start.2 = (f32[2,8,1,512]{3,2,1,0:T(1,128)S(1)}, f32[2,8,1,512]{3,2,1,0:T(1,128)S(1)}, u32[]{:S(2)}, u32[]{:S(2)}) collective-permute-start(f32[2,8,1,512]{3,2,1,0:T(1,128)S(1)} %pad_maximum_fusion.7), channel_id=1, source_target_pairs={{0,1},{1,2},{2,3},{3,4},{4,5},{5,6},{6,7},{8,9},{9,10},{10,11},{11... | collective-permute-start | bytes 98312 | tf_op jit(solution)/shard_map/ppermute | solution.py:18
  28.5 25.5 %collective-permute-start.3 = (f32[2,1,32,512]{3,2,1,0:T(8,128)}, f32[2,1,32,512]{3,2,1,0:T(8,128)}, u32[]{:S(2)}, u32[]{:S(2)}) collective-permute-start(f32[2,1,32,512]{3,2,1,0:T(8,128)} %pad_maximum_fusion.3), channel_id=1, source_target_pairs={{0,8},{8,16},{16,24},{1,9},{9,17},{17,25},{2,10},{10,18},{18,26},{... | collective-permute-start | bytes 393224 | tf_op jit(solution)/shard_map/ppermute | solution.py:18
  49.1 1.9 copy-start.1
  54.8 13.9 %copy-start.12 = (pred[8,32,512]{2,1,0:T(8,128)(4,1)S(1)}, pred[8,32,512]{2,1,0:T(8,128)(4,1)}, u32[]{:S(2)}) copy-start(pred[8,32,512]{2,1,0:T(8,128)(4,1)} %get-tuple-element.141) | copy-start | bytes 393220
  54.8 13.9 %copy-start.22 = (f32[7,32,512]{2,1,0:T(8,128)S(1)}, f32[7,32,512]{2,1,0:T(8,128)}, u32[]{:S(2)}) copy-start(f32[7,32,512]{2,1,0:T(8,128)} %slice.428) | copy-start | bytes 1376260
  67.9 0.8 copy-start.8
  68.7 16.2 %copy-start.27 = (f32[1,1,256]{2,1,0:T(1,128)S(1)}, f32[1,1,256]{2,1,0:T(1,128)}, u32[]{:S(2)}) copy-start(f32[1,1,256]{2,1,0:T(1,128)} %stack.239) | copy-start | bytes 3076
  68.7 16.2 %copy-start.28 = (f32[1,1,256]{2,1,0:T(1,128)S(1)}, f32[1,1,256]{2,1,0:T(1,128)}, u32[]{:S(2)}) copy-start(f32[1,1,256]{2,1,0:T(1,128)} %stack.238) | copy-start | bytes 3076
  68.7 16.2 %copy-start.29 = (f32[1,1,256]{2,1,0:T(1,128)S(1)}, f32[1,1,256]{2,1,0:T(1,128)}, u32[]{:S(2)}) copy-start(f32[1,1,256]{2,1,0:T(1,128)} %stack.241) | copy-start | bytes 3076
  81.5 0.8 copy-start.4
  81.5 6.6 %copy-start.9 = (f32[8,32,512]{2,1,0:T(8,128)S(1)}, f32[8,32,512]{2,1,0:T(8,128)}, u32[]{:S(2)}) copy-start(f32[8,32,512]{2,1,0:T(8,128)} %copy-done.8) | copy-start | bytes 1572868
  82.5 5.6 %copy-start.5 = (f32[8,32,512]{2,1,0:T(8,128)S(1)}, f32[8,32,512]{2,1,0:T(8,128)}, u32[]{:S(2)}) copy-start(f32[8,32,512]{2,1,0:T(8,128)} %copy-done.4) | copy-start | bytes 1572868
  82.5 7.0 %collective-permute-start.5 = (f32[2,8,1,512]{3,2,1,0:T(1,128)S(1)}, f32[2,8,1,512]{3,2,1,0:T(1,128)S(1)}, u32[]{:S(2)}, u32[]{:S(2)}) collective-permute-start(f32[2,8,1,512]{3,2,1,0:T(1,128)S(1)} %pad_maximum_fusion.8), channel_id=1, source_target_pairs={{1,0},{2,1},{3,2},{4,3},{5,4},{6,5},{7,6},{9,8},{10,9},{11,10},{12... | collective-permute-start | bytes 98312 | tf_op jit(solution)/shard_map/ppermute | solution.py:18
  85.5 9.8 %copy-start.2 = (f32[8,32,512]{2,1,0:T(8,128)S(1)}, f32[8,32,512]{2,1,0:T(8,128)}, u32[]{:S(2)}) copy-start(f32[8,32,512]{2,1,0:T(8,128)} %copy-done.1) | copy-start | bytes 1572868
  85.5 9.8 %copy-start.6 = (f32[8,32,512]{2,1,0:T(8,128)S(1)}, f32[8,32,512]{2,1,0:T(8,128)}, u32[]{:S(2)}) copy-start(f32[8,32,512]{2,1,0:T(8,128)} %copy-done.4) | copy-start | bytes 1572868
  85.5 9.8 %copy-start.10 = (f32[8,32,512]{2,1,0:T(8,128)S(1)}, f32[8,32,512]{2,1,0:T(8,128)}, u32[]{:S(2)}) copy-start(f32[8,32,512]{2,1,0:T(8,128)} %copy-done.8) | copy-start | bytes 1572868
  85.5 9.8 %copy-start.20 = (f32[8,31,512]{2,1,0:T(8,128)S(1)}, f32[8,31,512]{2,1,0:T(8,128)}, u32[]{:S(2)}) copy-start(f32[8,31,512]{2,1,0:T(8,128)} %slice.437) | copy-start | bytes 1523716
  85.6 9.8 %copy-start.21 = (f32[8,32,511]{2,1,0:T(8,128)S(1)}, f32[8,32,511]{2,1,0:T(8,128)}, u32[]{:S(2)}) copy-start(f32[8,32,511]{2,1,0:T(8,128)} %slice.448) | copy-start | bytes 1569796
  88.2 7.1 %collective-permute-start.4 = (f32[2,1,32,512]{3,2,1,0:T(8,128)S(1)}, f32[2,1,32,512]{3,2,1,0:T(8,128)S(1)}, u32[]{:S(2)}, u32[]{:S(2)}) collective-permute-start(f32[2,1,32,512]{3,2,1,0:T(8,128)S(1)} %pad_maximum_fusion.4), channel_id=1, source_target_pairs={{8,0},{16,8},{24,16},{9,1},{17,9},{25,17},{10,2},{18,10},{26,18},{... | collective-permute-start | bytes 393224 | tf_op jit(solution)/shard_map/ppermute | solution.py:18
  96.5 10.8 %collective-permute-start.6 = (f32[2,8,1,512]{3,2,1,0:T(1,128)S(1)}, f32[2,8,1,512]{3,2,1,0:T(1,128)S(1)}, u32[]{:S(2)}, u32[]{:S(2)}) collective-permute-start(f32[2,8,1,512]{3,2,1,0:T(1,128)S(1)} %pad_maximum_fusion.9), channel_id=1, source_target_pairs={{0,1},{1,2},{2,3},{3,4},{4,5},{5,6},{6,7},{8,9},{9,10},{10,11},{11... | collective-permute-start | bytes 98312 | tf_op jit(solution)/shard_map/ppermute | solution.py:18
  99.4 7.9 %copy-start.3 = (f32[8,32,512]{2,1,0:T(8,128)S(1)}, f32[8,32,512]{2,1,0:T(8,128)}, u32[]{:S(2)}) copy-start(f32[8,32,512]{2,1,0:T(8,128)} %copy-done.1) | copy-start | bytes 1572868
  99.4 7.9 %copy-start.13 = (pred[8,32,512]{2,1,0:T(8,128)(4,1)S(1)}, pred[8,32,512]{2,1,0:T(8,128)(4,1)}, u32[]{:S(2)}) copy-start(pred[8,32,512]{2,1,0:T(8,128)(4,1)} %get-tuple-element.141) | copy-start | bytes 393220
  102.3 18.9 %collective-permute-start.7 = (f32[2,1,32,512]{3,2,1,0:T(8,128)S(1)}, f32[2,1,32,512]{3,2,1,0:T(8,128)S(1)}, u32[]{:S(2)}, u32[]{:S(2)}) collective-permute-start(f32[2,1,32,512]{3,2,1,0:T(8,128)S(1)} %pad_maximum_fusion.5), channel_id=1, source_target_pairs={{0,8},{8,16},{16,24},{1,9},{9,17},{17,25},{2,10},{10,18},{18,26},{... | collective-permute-start | bytes 393224 | tf_op jit(solution)/shard_map/ppermute | solution.py:18
  107.3 13.9 %copy-start.7 = (f32[8,32,512]{2,1,0:T(8,128)S(1)}, f32[8,32,512]{2,1,0:T(8,128)}, u32[]{:S(2)}) copy-start(f32[8,32,512]{2,1,0:T(8,128)} %copy-done.4) | copy-start | bytes 1572868
  120.2 0.8 copy-start.14
  121.2 13.2 %copy-start.25 = (f32[1,4,256]{2,1,0:T(4,128)S(1)}, f32[1,4,256]{2,1,0:T(4,128)}, u32[]{:S(2)}) copy-start(f32[1,4,256]{2,1,0:T(4,128)} %get-tuple-element.200) | copy-start | bytes 12292
  121.2 13.2 %copy-start.26 = (f32[1,4,256]{2,1,0:T(4,128)S(1)}, f32[1,4,256]{2,1,0:T(4,128)}, u32[]{:S(2)}) copy-start(f32[1,4,256]{2,1,0:T(4,128)} %get-tuple-element.202) | copy-start | bytes 12292
  121.2 13.2 %copy-start.23 = (f32[1,4,256]{2,1,0:T(4,128)S(1)}, f32[1,4,256]{2,1,0:T(4,128)}, u32[]{:S(2)}) copy-start(f32[1,4,256]{2,1,0:T(4,128)} %get-tuple-element.199) | copy-start | bytes 12292
  121.3 13.2 %copy-start.24 = (f32[1,4,256]{2,1,0:T(4,128)S(1)}, f32[1,4,256]{2,1,0:T(4,128)}, u32[]{:S(2)}) copy-start(f32[1,4,256]{2,1,0:T(4,128)} %get-tuple-element.201) | copy-start | bytes 12292
  121.3 13.2 %copy-start.34 = (s32[8]{0:T(128)S(1)}, s32[8]{0:T(128)}, u32[]{:S(2)}) copy-start(s32[8]{0:T(128)} %iota_multiply_fusion) | copy-start | bytes 100
  134.2 0.8 copy-start.16
  257.4 2.5 copy-start.11
  259.9 12.3 %copy-start.15 = (f32[8,32,512]{2,1,0:T(8,128)S(1)}, f32[8,32,512]{2,1,0:T(8,128)}, u32[]{:S(2)}) copy-start(f32[8,32,512]{2,1,0:T(8,128)} %copy-done.14) | copy-start | bytes 1572868
  259.9 12.3 %copy-start.17 = (f32[8,32,512]{2,1,0:T(8,128)S(1)}, f32[8,32,512]{2,1,0:T(8,128)}, u32[]{:S(2)}) copy-start(f32[8,32,512]{2,1,0:T(8,128)} %copy-done.16) | copy-start | bytes 1572868
  272.2 1.3 copy-start.18
  272.2 1.5 copy-start.19
Sparse Core Ops, SparseCore 0:
  260.0 129.8 all-reduce.9
where the time goes:
time: 401 us; the launch traced here: 399 us
  other arithmetic  132 us (33%)
  waiting for transfers between devices  121 us (30%)
  matrix products  76.3 us (19%)
  local copies, waits for them, and re-layouts  32.3 us (8%)
  starting transfers between devices  22.1 us (6%)
  between operations  15.5 us (4%)
    psum x1, waiting for transfers between devices, shards(): total = lax.psum(partial_far, ('gx', 'gy'))  115 us
    add x5, other arithmetic, shards(): fields[i] + (DT * curls[i] - (newpol[i] - pols[i])) * vox_inv  64.9 us
    ppermute x8, starting transfers between devices, shifted(): return lax.ppermute(shard, axis, pairs)  22.1 us
    dot_general x16, matrix products, project(): jnp.dot(real_flat[f], cosine, precision=hi)  19.1 us
    dot_general x16, matrix products, project(): jnp.dot(imag_flat[f], cosine, precision=hi)  19.1 us
    dot_general x16, matrix products, project(): jnp.dot(imag_flat[f], sine, precision=hi)  19.1 us
    dot_general x16, matrix products, project(): jnp.dot(real_flat[f], sine, precision=hi)  19 us
    cos x8, other arithmetic, project(): cos_y = jnp.cos(along_y)  15.1 us
  transfers between devices with their start and end apart: 9, of which 2 were waited for; matrix products, arithmetic and copies ran while one was open for 16% of the time, Pallas kernels for 0%

commit v1 on v0

--- a/solution.py
+++ b/solution.py
@@ -187,7 +187,7 @@
         jnp.float32
     )
     partial_far = project_cells(real_acc, imag_acc, xglobal, yglobal, 0, NDIR)
-    total = lax.psum(partial_far, ("gx", "gy"))
+    total = lax.psum(lax.psum(partial_far, "gy"), "gx")
     grid_x = cells_x * lax.axis_size("gx")
     grid_y = cells_y * lax.axis_size("gy")
     far_field = total * (1.0 / math.sqrt(grid_x * grid_y))

time: 401 us -> 382 us (0.953)
  waiting for transfers between devices: 121 us -> 103 us
    psum x1 -> x2, waiting for transfers between devices: 115 us -> 97.3 us  [shards(): total = lax.psum(lax.psum(partial_far, 'gy'), 'gx')]
  transfers between devices with their start and end apart: 9 -> 10, of which waited for: 2 -> 3; matrix products, arithmetic and copies ran while one was open for 16% -> 17% of each run, Pallas kernels for 0% -> 0%
where the time goes in v1:
time: 382 us; the launch traced here: 380 us
  other arithmetic  132 us (35%)
  waiting for transfers between devices  103 us (27%)
  matrix products  76.3 us (20%)
  local copies, waits for them, and re-layouts  30.5 us (8%)
  starting transfers between devices  22.2 us (6%)
  between operations  15.4 us (4%)
    psum x2, waiting for transfers between devices, shards(): total = lax.psum(lax.psum(partial_far, 'gy'), 'gx')  97.3 us
    add x5, other arithmetic, shards(): fields[i] + (DT * curls[i] - (newpol[i] - pols[i])) * vox_inv  65.3 us
    ppermute x8, starting transfers between devices, shifted(): return lax.ppermute(shard, axis, pairs)  22.1 us
    dot_general x16, matrix products, project(): jnp.dot(real_flat[f], cosine, precision=hi)  19.1 us
    dot_general x16, matrix products, project(): jnp.dot(imag_flat[f], sine, precision=hi)  19.1 us
    dot_general x16, matrix products, project(): jnp.dot(imag_flat[f], cosine, precision=hi)  19.1 us
    dot_general x16, matrix products, project(): jnp.dot(real_flat[f], sine, precision=hi)  19 us
    cos x8, other arithmetic, project(): cos_y = jnp.cos(along_y)  15.1 us
  transfers between devices with their start and end apart: 10, of which 3 were waited for; matrix products, arithmetic and copies ran while one was open for 17% of the time, Pallas kernels for 0%

profile of v1, /device:TPU:0, one launch (start us, length us, event | category | flops | bytes accessed | tf_op | source)
XLA Modules:
  0.0 380.4 jit_solution(4233388220097985972)
XLA Ops:
  7.3 1.6 slice_bitcast_fusion.1
  9.0 1.3 collective-permute-start.1
  10.3 1.3 collective-permute-start
  19.7 3.1 fusion.46
  23.1 3.0 collective-permute-start.2
  28.4 6.1 %collective-permute-start.3 = (f32[2,1,32,512]{3,2,1,0:T(8,128)}, f32[2,1,32,512]{3,2,1,0:T(8,128)}, u32[]{:S(2)}, u32[]{:S(2)}) collective-permute-start(f32[2,1,32,512]{3,2,1,0:T(8,128)} %pad_maximum_fusion.3), channel_id=1, source_target_pairs={{0,8},{8,16},{16,24},{1,9},{9,17},{17,25},{2,10},{10,18},{18,26},{... | collective-permute-start | bytes 393224 | tf_op jit(solution)/shard_map/ppermute | solution.py:18
  35.8 13.2 %fusion.51 = (f32[8,32,512]{2,1,0:T(8,128)S(1)}, f32[8,32,512]{2,1,0:T(8,128)}, pred[8,32,512]{2,1,0:T(8,128)(4,1)S(1)}, pred[8,32,512]{2,1,0:T(8,128)(4,1)S(1)}...) fusion(f32[8,32,512]{2,1,0:T(8,128)S(1)} %get-tuple-element.169, f32[8,31,512]{2,1,0:T(8,128)S(1)} %bitcast.335, ...), kind=kLoop, calls=%fused_computation.90 | loop fusion | flops 6029312 | bytes 5766208 | tf_op jit(solution)/shard_map/add | solution.py:171
  51.8 1.3 stack.241
  54.9 13.1 %fusion.64 = (f32[8,32,512]{2,1,0:T(8,128)S(1)}, f32[8,32,512]{2,1,0:T(8,128)}) fusion(f32[8,32,512]{2,1,0:T(8,128)S(1)} %get-tuple-element.170, f32[7,32,512]{2,1,0:T(8,128)} %slice.432, f32[1,32,512]{2,1,0:T(8,128)S(1)} %get-tuple-element.184, f32[8,32,512]{2,1,0:T(8,128)S(1)} %get-tuple-element.168, f32[8,31,512]{2,1,0:T(8,128)S(1)} %bitcast.328, ...), kind=kLoop, calls=%fused_computation.106 | loop fusion | flops 5636096 | bytes 5242944 | tf_op jit(solution)/shard_map/add | solution.py:171
  68.8 12.9 %fusion.59 = (f32[8,32,512]{2,1,0:T(8,128)S(1)}, f32[8,32,512]{2,1,0:T(8,128)}) fusion(f32[8,32,512]{2,1,0:T(8,128)S(1)} %get-tuple-element.169, f32[7,32,512]{2,1,0:T(8,128)S(1)} %copy-done.21, f32[1,32,512]{2,1,0:T(8,128)S(1)} %get-tuple-element.183, f32[8,32,512]{2,1,0:T(8,128)S(1)} %get-tuple-element.168, f32[8,32,511]{2,1,0:T(8,128)S(1)} %bitcast.329, ...), kind=kLoop, calls=%fused_computation.100 | loop fusion | flops 5505024 | bytes 5241920 | tf_op jit(solution)/shard_map/add | solution.py:171
  82.7 1.4 collective-permute-start.5
  85.8 1.3 slice.441
  87.1 1.2 slice.443
  88.4 1.3 collective-permute-start.4
  89.7 5.8 %collective-permute-done.4 = f32[2,1,32,512]{3,2,1,0:T(8,128)S(1)} collective-permute-done((f32[2,1,32,512]{3,2,1,0:T(8,128)S(1)}, f32[2,1,32,512]{3,2,1,0:T(8,128)S(1)}, u32[]{:S(2)}, u32[]{:S(2)}) %collective-permute-start.4) | collective-permute-done | bytes 131104 | tf_op jit(solution)/shard_map/ppermute | solution.py:18
  96.8 2.8 collective-permute-start.6
  100.4 4.8 %collective-permute-start.7 = (f32[2,1,32,512]{3,2,1,0:T(8,128)S(1)}, f32[2,1,32,512]{3,2,1,0:T(8,128)S(1)}, u32[]{:S(2)}, u32[]{:S(2)}) collective-permute-start(f32[2,1,32,512]{3,2,1,0:T(8,128)S(1)} %pad_maximum_fusion.5), channel_id=1, source_target_pairs={{0,8},{8,16},{16,24},{1,9},{9,17},{17,25},{2,10},{10,18},{18,26},{... | collective-permute-start | bytes 393224 | tf_op jit(solution)/shard_map/ppermute | solution.py:18
  105.4 13.1 %fusion.75 = (f32[8,32,512]{2,1,0:T(8,128)S(1)}, f32[8,32,512]{2,1,0:T(8,128)}) fusion(f32[8,32,512]{2,1,0:T(8,128)S(1)} %copy-done.3, f32[8,32,512]{2,1,0:T(8,128)S(1)} %get-tuple-element.177, f32[8,31,512]{2,1,0:T(8,128)S(1)} %bitcast.333, f32[8,1,512]{2,1,0:T(1,128)S(1)} %get-tuple-element.187, f32[8,32,512]{2,1,0:T(8,128)} %get-tuple-element.137, ...), kind=kLoop, calls=%fused_computation.122 | loop fusion | flops 5505024 | bytes 5241920 | tf_op jit(solution)/shard_map/add | solution.py:171
  119.5 13.0 %fusion.83 = (f32[8,32,512]{2,1,0:T(8,128)S(1)}, f32[8,32,512]{2,1,0:T(8,128)}) fusion(f32[8,32,512]{2,1,0:T(8,128)S(1)} %copy-done.7, f32[8,32,512]{2,1,0:T(8,128)S(1)} %get-tuple-element.177, f32[7,32,512]{2,1,0:T(8,128)} %slice.456, f32[1,32,512]{2,1,0:T(8,128)S(1)} %get-tuple-element.179, f32[8,32,512]{2,1,0:T(8,128)} %get-tuple-element.143, ...), kind=kLoop, calls=%fused_computation.132 | loop fusion | flops 5505024 | bytes 5241920 | tf_op jit(solution)/shard_map/add | solution.py:171
  132.8 122.4 %while.13 = (s32[]{:T(128)}, f32[8,2,2,4,2048]{4,3,2,1,0:T(4,128)}, s32[8]{0:T(128)S(1)}, f32[2,4,256]{2,1,0:T(4,128)S(1)}, f32[2,4,256]{2,1,0:T(4,128)S(1)}, /*index=5*/s32[]{:T(128)}, s32[]{:T(128)}, s32[]{:T(128)}) while((s32[]{:T(128)}, f32[8,2,2,4,2048]{4,3,2,1,0:T(4,128)}, s32[8]{0:T(128)S(1)}, f32[2,4,256]{2,1,0:T(4,128)S(1)}, ...), condition=%wide.region_1.2_spmd.clone, body=%wide.region_0.1_spmd.clone.sunk | while | flops 207937696 | bytes 28771064 | solution.py:128
  134.3 1.9 multiply_cosine_fusion.6
  138.5 1.2 fusion.167
  139.7 1.2 fusion.168
  140.9 1.2 fusion.169
  143.9 1.2 fusion.171
  145.1 1.2 fusion.172
  146.3 1.2 fusion.173
  149.6 1.9 multiply_cosine_fusion.6
  153.8 1.2 fusion.167
  155.0 1.2 fusion.168
  156.2 1.2 fusion.169
  159.2 1.2 fusion.171
  160.4 1.2 fusion.172
  161.6 1.2 fusion.173
  164.8 1.9 multiply_cosine_fusion.6
  169.1 1.2 fusion.167
  170.3 1.2 fusion.168
  171.5 1.2 fusion.169
  174.5 1.2 fusion.171
  175.7 1.2 fusion.172
  180.1 1.9 multiply_cosine_fusion.6
  185.5 1.2 fusion.168
  190.9 1.2 fusion.172
  195.4 1.9 multiply_cosine_fusion.6
  200.8 1.2 fusion.168
  206.2 1.2 fusion.172
  210.6 1.9 multiply_cosine_fusion.6
  216.1 1.2 fusion.168
  221.5 1.2 fusion.172
  225.9 1.9 multiply_cosine_fusion.6
  231.3 1.2 fusion.168
  236.7 1.2 fusion.172
  241.2 1.9 multiply_cosine_fusion.6
  246.6 1.2 fusion.168
  252.0 1.2 fusion.172
  253.2 1.2 fusion.173
  255.1 2.3 copy.16
  257.5 59.0 %all-reduce.11.cloned.1.call-done = f32[2,2,4,16384]{3,2,1,0:T(4,128)} async-done(((f32[2,2,4,16384]{3,2,1,0:T(4,128)}), f32[2,2,4,16384]{3,2,1,0:T(4,128)}) %all-reduce.11.cloned.1.call-update) | async-done | bytes 1048592 | tf_op jit(solution)/shard_map/psum | solution.py:190
  316.6 1.3 pad_maximum_fusion.1
  317.9 12.0 %fusion.89 = (f32[1,8,32,512]{3,2,1,0:T(8,128)S(1)}, f32[8,32,512]{2,1,0:T(8,128)S(1)}) fusion(f32[8,32,512]{2,1,0:T(8,128)S(1)} %copy-done.11, f32[8,32,512]{2,1,0:T(8,128)S(1)} %get-tuple-element.178, f32[7,32,512]{2,1,0:T(8,128)S(1)} %slice.458, f32[1,32,512]{2,1,0:T(8,128)S(1)} %get-tuple-element.180, f32[8,32,512]{2,1,0:T(8,128)S(1)} %get-tuple-element.176, ...), kind=kLoop, calls=%fused_computation.139 | loop fusion | flops 5636096 | bytes 5242944 | tf_op jit(solution)/shard_map/stack | solution.py:194
  329.9 1.3 pad_maximum_fusion
  331.4 1.3 pad_maximum_fusion.2
  332.7 38.4 %all-reduce.13.cloned.1.call-done = f32[2,2,4,16384]{3,2,1,0:T(4,128)} async-done(((f32[2,2,4,16384]{3,2,1,0:T(4,128)}), f32[2,2,4,16384]{3,2,1,0:T(4,128)}) %all-reduce.13.cloned.1.call-update) | async-done | bytes 1048592 | tf_op jit(solution)/shard_map/psum | solution.py:190
  371.1 2.5 broadcast_multiply_fusion
  (250 shorter events, 96.1 us)
Async XLA Ops:
  7.2 3.1 copy-start
  7.2 5.5 %copy-start.25 = (f32[4]{0:T(128)S(1)}, f32[4]{0:T(128)}, u32[]{:S(2)}) copy-start(f32[4]{0:T(128)} %param.17) | copy-start | bytes 52
  7.2 6.1 %copy-start.22 = (f32[4]{0:T(128)S(1)}, f32[4]{0:T(128)}, u32[]{:S(2)}) copy-start(f32[4]{0:T(128)} %param.19) | copy-start | bytes 52
  7.2 6.1 %copy-start.23 = (f32[4]{0:T(128)S(1)}, f32[4]{0:T(128)}, u32[]{:S(2)}) copy-start(f32[4]{0:T(128)} %param.20) | copy-start | bytes 52
  7.2 6.1 %copy-start.24 = (f32[4]{0:T(128)S(1)}, f32[4]{0:T(128)}, u32[]{:S(2)}) copy-start(f32[4]{0:T(128)} %param.18) | copy-start | bytes 52
  7.2 309.3 %all-reduce.11.cloned.1.call-start = ((), (), s32[]{:S(2)}) async-start(), calls=%async_computation | async-start | bytes 2097152 | tf_op jit(solution)/shard_map/psum | solution.py:190
  9.0 10.7 %collective-permute-start.1 = (f32[2,8,1,512]{3,2,1,0:T(1,128)S(1)}, f32[2,8,1,512]{3,2,1,0:T(1,128)S(1)}, u32[]{:S(2)}, u32[]{:S(2)}) collective-permute-start(f32[2,8,1,512]{3,2,1,0:T(1,128)S(1)} %pad_maximum_fusion.6), channel_id=1, source_target_pairs={{1,0},{2,1},{3,2},{4,3},{5,4},{6,5},{7,6},{9,8},{10,9},{11,10},{12... | collective-permute-start | bytes 98312 | tf_op jit(solution)/shard_map/ppermute | solution.py:18
  10.3 9.4 %collective-permute-start = (f32[2,1,32,512]{3,2,1,0:T(8,128)S(1)}, f32[2,1,32,512]{3,2,1,0:T(8,128)S(1)}, u32[]{:S(2)}, u32[]{:S(2)}) collective-permute-start(f32[2,1,32,512]{3,2,1,0:T(8,128)S(1)} %stack.204), channel_id=1, source_target_pairs={{8,0},{16,8},{24,16},{9,1},{17,9},{25,17},{10,2},{18,10},{26,18},{... | collective-permute-start | bytes 393224 | tf_op jit(solution)/shard_map/ppermute | solution.py:18
  23.1 12.8 %collective-permute-start.2 = (f32[2,8,1,512]{3,2,1,0:T(1,128)S(1)}, f32[2,8,1,512]{3,2,1,0:T(1,128)S(1)}, u32[]{:S(2)}, u32[]{:S(2)}) collective-permute-start(f32[2,8,1,512]{3,2,1,0:T(1,128)S(1)} %pad_maximum_fusion.7), channel_id=1, source_target_pairs={{0,1},{1,2},{2,3},{3,4},{4,5},{5,6},{6,7},{8,9},{9,10},{10,11},{11... | collective-permute-start | bytes 98312 | tf_op jit(solution)/shard_map/ppermute | solution.py:18
  28.4 25.6 %collective-permute-start.3 = (f32[2,1,32,512]{3,2,1,0:T(8,128)}, f32[2,1,32,512]{3,2,1,0:T(8,128)}, u32[]{:S(2)}, u32[]{:S(2)}) collective-permute-start(f32[2,1,32,512]{3,2,1,0:T(8,128)} %pad_maximum_fusion.3), channel_id=1, source_target_pairs={{0,8},{8,16},{16,24},{1,9},{9,17},{17,25},{2,10},{10,18},{18,26},{... | collective-permute-start | bytes 393224 | tf_op jit(solution)/shard_map/ppermute | solution.py:18
  49.1 2.0 copy-start.1
  54.9 13.9 %copy-start.12 = (pred[8,32,512]{2,1,0:T(8,128)(4,1)S(1)}, pred[8,32,512]{2,1,0:T(8,128)(4,1)}, u32[]{:S(2)}) copy-start(pred[8,32,512]{2,1,0:T(8,128)(4,1)} %get-tuple-element.141) | copy-start | bytes 393220
  54.9 13.9 %copy-start.21 = (f32[7,32,512]{2,1,0:T(8,128)S(1)}, f32[7,32,512]{2,1,0:T(8,128)}, u32[]{:S(2)}) copy-start(f32[7,32,512]{2,1,0:T(8,128)} %slice.428) | copy-start | bytes 1376260
  68.0 0.8 copy-start.8
  81.7 0.8 copy-start.4
  81.7 6.7 %copy-start.9 = (f32[8,32,512]{2,1,0:T(8,128)S(1)}, f32[8,32,512]{2,1,0:T(8,128)}, u32[]{:S(2)}) copy-start(f32[8,32,512]{2,1,0:T(8,128)} %copy-done.8) | copy-start | bytes 1572868
  82.6 5.7 %copy-start.5 = (f32[8,32,512]{2,1,0:T(8,128)S(1)}, f32[8,32,512]{2,1,0:T(8,128)}, u32[]{:S(2)}) copy-start(f32[8,32,512]{2,1,0:T(8,128)} %copy-done.4) | copy-start | bytes 1572868
  82.7 7.0 %collective-permute-start.5 = (f32[2,8,1,512]{3,2,1,0:T(1,128)S(1)}, f32[2,8,1,512]{3,2,1,0:T(1,128)S(1)}, u32[]{:S(2)}, u32[]{:S(2)}) collective-permute-start(f32[2,8,1,512]{3,2,1,0:T(1,128)S(1)} %pad_maximum_fusion.8), channel_id=1, source_target_pairs={{1,0},{2,1},{3,2},{4,3},{5,4},{6,5},{7,6},{9,8},{10,9},{11,10},{12... | collective-permute-start | bytes 98312 | tf_op jit(solution)/shard_map/ppermute | solution.py:18
  85.8 9.8 %copy-start.2 = (f32[8,32,512]{2,1,0:T(8,128)S(1)}, f32[8,32,512]{2,1,0:T(8,128)}, u32[]{:S(2)}) copy-start(f32[8,32,512]{2,1,0:T(8,128)} %copy-done.1) | copy-start | bytes 1572868
  85.8 9.8 %copy-start.6 = (f32[8,32,512]{2,1,0:T(8,128)S(1)}, f32[8,32,512]{2,1,0:T(8,128)}, u32[]{:S(2)}) copy-start(f32[8,32,512]{2,1,0:T(8,128)} %copy-done.4) | copy-start | bytes 1572868
  85.8 9.8 %copy-start.10 = (f32[8,32,512]{2,1,0:T(8,128)S(1)}, f32[8,32,512]{2,1,0:T(8,128)}, u32[]{:S(2)}) copy-start(f32[8,32,512]{2,1,0:T(8,128)} %copy-done.8) | copy-start | bytes 1572868
  85.8 9.8 %copy-start.19 = (f32[8,31,512]{2,1,0:T(8,128)S(1)}, f32[8,31,512]{2,1,0:T(8,128)}, u32[]{:S(2)}) copy-start(f32[8,31,512]{2,1,0:T(8,128)} %slice.437) | copy-start | bytes 1523716
  85.8 9.8 %copy-start.20 = (f32[8,32,511]{2,1,0:T(8,128)S(1)}, f32[8,32,511]{2,1,0:T(8,128)}, u32[]{:S(2)}) copy-start(f32[8,32,511]{2,1,0:T(8,128)} %slice.448) | copy-start | bytes 1569796
  88.4 7.2 %collective-permute-start.4 = (f32[2,1,32,512]{3,2,1,0:T(8,128)S(1)}, f32[2,1,32,512]{3,2,1,0:T(8,128)S(1)}, u32[]{:S(2)}, u32[]{:S(2)}) collective-permute-start(f32[2,1,32,512]{3,2,1,0:T(8,128)S(1)} %pad_maximum_fusion.4), channel_id=1, source_target_pairs={{8,0},{16,8},{24,16},{9,1},{17,9},{25,17},{10,2},{18,10},{26,18},{... | collective-permute-start | bytes 393224 | tf_op jit(solution)/shard_map/ppermute | solution.py:18
  96.4 9.0 %copy-start.3 = (f32[8,32,512]{2,1,0:T(8,128)S(1)}, f32[8,32,512]{2,1,0:T(8,128)}, u32[]{:S(2)}) copy-start(f32[8,32,512]{2,1,0:T(8,128)} %copy-done.1) | copy-start | bytes 1572868
  96.8 8.6 %collective-permute-start.6 = (f32[2,8,1,512]{3,2,1,0:T(1,128)S(1)}, f32[2,8,1,512]{3,2,1,0:T(1,128)S(1)}, u32[]{:S(2)}, u32[]{:S(2)}) collective-permute-start(f32[2,8,1,512]{3,2,1,0:T(1,128)S(1)} %pad_maximum_fusion.9), channel_id=1, source_target_pairs={{0,1},{1,2},{2,3},{3,4},{4,5},{5,6},{6,7},{8,9},{9,10},{10,11},{11... | collective-permute-start | bytes 98312 | tf_op jit(solution)/shard_map/ppermute | solution.py:18
  100.4 19.0 %collective-permute-start.7 = (f32[2,1,32,512]{3,2,1,0:T(8,128)S(1)}, f32[2,1,32,512]{3,2,1,0:T(8,128)S(1)}, u32[]{:S(2)}, u32[]{:S(2)}) collective-permute-start(f32[2,1,32,512]{3,2,1,0:T(8,128)S(1)} %pad_maximum_fusion.5), channel_id=1, source_target_pairs={{0,8},{8,16},{16,24},{1,9},{9,17},{17,25},{2,10},{10,18},{18,26},{... | collective-permute-start | bytes 393224 | tf_op jit(solution)/shard_map/ppermute | solution.py:18
  105.4 14.1 %copy-start.7 = (f32[8,32,512]{2,1,0:T(8,128)S(1)}, f32[8,32,512]{2,1,0:T(8,128)}, u32[]{:S(2)}) copy-start(f32[8,32,512]{2,1,0:T(8,128)} %copy-done.4) | copy-start | bytes 1572868
  105.4 14.1 %copy-start.13 = (pred[8,32,512]{2,1,0:T(8,128)(4,1)S(1)}, pred[8,32,512]{2,1,0:T(8,128)(4,1)}, u32[]{:S(2)}) copy-start(pred[8,32,512]{2,1,0:T(8,128)(4,1)} %get-tuple-element.141) | copy-start | bytes 393220
  118.5 0.8 copy-start.14
  119.5 13.2 %copy-start.26 = (s32[8]{0:T(128)S(1)}, s32[8]{0:T(128)}, u32[]{:S(2)}) copy-start(s32[8]{0:T(128)} %iota_multiply_fusion) | copy-start | bytes 100
  257.5 113.6 %all-reduce.13.cloned.1.call-start = ((), (), s32[]{:S(2)}) async-start(), calls=%async_computation.1 | async-start | bytes 2097152 | tf_op jit(solution)/shard_map/psum | solution.py:190
  316.5 1.4 copy-start.11
  316.5 1.4 copy-start.16
  317.9 12.0 %copy-start.15 = (f32[8,32,512]{2,1,0:T(8,128)S(1)}, f32[8,32,512]{2,1,0:T(8,128)}, u32[]{:S(2)}) copy-start(f32[8,32,512]{2,1,0:T(8,128)} %copy-done.14) | copy-start | bytes 1572868
  329.9 1.3 copy-start.17
  329.9 1.5 copy-start.18
Sparse Core Ops, SparseCore 0:
  257.6 58.8 all-reduce.10
  319.5 51.4 all-reduce.12
